TPU v7x, 32 devices: a whole 2x2x4 slice. The times are simulated.
32 devices in a mesh: dp: 4 (over y, x), chan: 8 (over z, core).
Axes of the slice: x: 2, y: 2, z: 4, core: 2. Of those that a mesh axis runs over, the one named last changes fastest.
Arguments:
- hidden_in: bfloat16 [4096, 8192], P('dp'), may hold values from -6 to 6
- proj_weight: bfloat16 [8192, 4096], P('dp', 'chan'), may hold values from -0.09375 to 0.09375
- embed: bfloat16 [4096, 4096], P('dp', 'chan')
- embed_grad: bfloat16 [4096, 4096], P('dp', 'chan')
- eigvec: float32 [4096, 512], P('chan'), as said below
- eigval: float32 [4096], P('chan'), as said below
Outputs:
- grad_weight: bfloat16 [8192, 4096], P('dp', 'chan')
- grad_hidden: bfloat16 [4096, 8192], P('dp', 'chan')
Inputs may be any that keep to these rules, and one draw needn't show every extreme that they name: `eigvec`: each group's block of 512 consecutive rows is an orthogonal matrix whose columns are that group's saved eigenvectors. `eigval`: each group's 512 saved eigenvalues are positive and any two of them differ by at least one percent of the larger.
All inputs are finite; a program needn't handle non-finite values.
Results may differ from a plain program's by a relative error of at most 0.005.
Values may be sent and summed in bfloat16 or wider, within the bound.
A program may use at most 192 MiB of HBM per device.

v0:
```python
import jax
import jax.numpy as jnp
from jax import lax
from jax.sharding import PartitionSpec as P

HI = lax.Precision.HIGHEST


def local(hidden_in, proj_weight, embed, embed_grad, eigvec, eigval):
    rows = embed.shape[0] * lax.axis_size("dp")
    zlocal = embed.astype(jnp.float32)
    glocal = embed_grad.astype(jnp.float32)
    sums_z, sums_g = lax.psum((jnp.sum(zlocal, axis=0), jnp.sum(glocal, axis=0)), "dp")
    mean_z = sums_z / rows
    mean_g = sums_g / rows
    centered = zlocal - mean_z
    local_moment = jnp.dot(centered.T, glocal, precision=HI, preferred_element_type=jnp.float32)
    dmat = lax.psum(local_moment, "dp")
    sym = 0.5 * (dmat + dmat.T)
    root = jnp.sqrt(eigval)
    whiten = jnp.dot(
        eigvec / root[None, :], eigvec.T, precision=HI, preferred_element_type=jnp.float32
    )
    loewner = -1.0 / (root[:, None] * root[None, :] * (root[:, None] + root[None, :]))
    half_rot = jnp.dot(eigvec.T, sym, precision=HI, preferred_element_type=jnp.float32)
    rotated = jnp.dot(half_rot, eigvec, precision=HI, preferred_element_type=jnp.float32)
    half_back = jnp.dot(eigvec, loewner * rotated, precision=HI, preferred_element_type=jnp.float32)
    dsigma = jnp.dot(half_back, eigvec.T, precision=HI, preferred_element_type=jnp.float32)
    first = jnp.dot(glocal - mean_g, whiten, precision=HI, preferred_element_type=jnp.float32)
    second = jnp.dot(centered, dsigma, precision=HI, preferred_element_type=jnp.float32)
    grad_z = (first + 2.0 / rows * second).astype(jnp.bfloat16)
    grad_weight = lax.psum_scatter(
        lax.dot_general(
            hidden_in, grad_z, (((0,), (0,)), ((), ())), preferred_element_type=jnp.float32
        ),
        "dp",
        scatter_dimension=0,
        tiled=True,
    ).astype(jnp.bfloat16)
    partial_input = lax.dot_general(
        grad_z,
        lax.all_gather(proj_weight, "dp", axis=0, tiled=True),
        (((1,), (1,)), ((), ())),
        preferred_element_type=jnp.float32,
    )
    grad_hidden = lax.psum_scatter(partial_input, "chan", scatter_dimension=1, tiled=True).astype(
        jnp.bfloat16
    )
    return (grad_weight, grad_hidden)


def solution(mesh):
    in_specs = (
        P("dp", None),
        P("dp", "chan"),
        P("dp", "chan"),
        P("dp", "chan"),
        P("chan", None),
        P("chan"),
    )
    out_specs = (P("dp", "chan"), P("dp", "chan"))
    return jax.shard_map(local, mesh=mesh, in_specs=in_specs, out_specs=out_specs, check_vma=False)
```

profile of v0, /device:TPU:0, one launch (start us, length us, event | category | flops | bytes accessed | tf_op | source)
XLA Modules:
  0.0 660.1 jit_solution(14970911284952542970)
XLA Ops:
  7.2 2.0 convert_reduce_fusion
  9.2 11.4 %all-reduce = (f32[512]{0:T(512)S(1)}, f32[512]{0:T(512)S(1)}) all-reduce(f32[512]{0:T(512)S(1)} %get-tuple-element.6, f32[512]{0:T(512)S(1)} %get-tuple-element.7), channel_id=1, replica_groups=mesh['dp'=4,'chan'=8] {'dp'}, use_global_device_ids=true, to_apply=%region_3.0 | all-reduce | flops 1024 | bytes 8192 | tf_op jit(solution)/shard_map/psum | solution.py:13
  20.6 2.8 fusion.1
  23.5 0.7 all-gather.2.cloned.1.call-update
  24.2 0.2 reduce-scatter.3.cloned.1.call-start
  24.5 0.2 copy-done
  24.7 2.8 fusion.3
  27.5 48.0 %all-reduce.3.cloned.1.call-done = f32[512,512]{1,0:T(8,128)} async-done(((f32[512,512]{1,0:T(8,128)}), f32[512,512]{1,0:T(8,128)}) %all-reduce.3.cloned.1.call-update) | async-done | bytes 1048592 | tf_op jit(solution)/shard_map/psum | solution.py:18
  75.5 2.5 copy.8
  78.1 3.5 fusion.6
  81.5 2.0 convolution_multiply_fusion
  83.5 3.5 fusion.14
  87.0 3.7 fusion.15
  90.7 3.5 fusion
  94.3 3.6 add_convert_fusion
  97.8 15.7 %convolution_bitcast_fusion = f32[8192,512]{0,1:T(8,128)} fusion(bf16[1024,512]{1,0:T(8,128)(2,1)S(1)} %add_convert_fusion, bf16[1024,8192]{1,0:T(8,128)(2,1)} %param.6), kind=kOutput, calls=%fused_computation | convolution fusion | flops 8589934592 | bytes 34603008 | tf_op jit(solution)/shard_map/dot_general | solution.py:33
  113.6 0.3 reduce-scatter.5.cloned.1.call-start
  113.9 51.1 %all-gather.2.cloned.1.call-done = bf16[8192,512]{1,0:T(8,128)(2,1)} async-done(((bf16[2048,512]{1,0:T(8,128)(2,1)}), bf16[8192,512]{1,0:T(8,128)(2,1)}) %all-gather.2.cloned.1.call-update) | async-done | bytes 8388624 | tf_op jit(solution)/shard_map/all_gather | solution.py:42
  165.0 18.2 %fusion.16 = f32[1024,8192]{1,0:T(8,128)} fusion(bf16[1024,512]{1,0:T(8,128)(2,1)S(1)} %add_convert_fusion, bf16[8192,512]{1,0:T(8,128)(2,1)} %all-gather.2.cloned.1.call-done), kind=kOutput, calls=%fused_computation.25 | convolution fusion | flops 8589934592 | bytes 42991616 | tf_op jit(solution)/shard_map/dot_general | solution.py:40
  183.3 138.7 %reduce-scatter.3.cloned.1.call-done = f32[2048,512]{0,1:T(8,128)} async-done(((f32[8192,512]{0,1:T(8,128)}), f32[2048,512]{0,1:T(8,128)}) %reduce-scatter.3.cloned.1.call-update) | async-done | bytes 4194320 | tf_op jit(solution)/shard_map/reduce_scatter | solution.py:32
  322.0 2.5 convert_element_type.18
  324.5 2.5 copy.9
  327.0 322.8 %reduce-scatter.5.cloned.1.call-done = f32[1024,1024]{1,0:T(8,128)} async-done(((f32[1024,8192]{1,0:T(8,128)}), f32[1024,1024]{1,0:T(8,128)}) %reduce-scatter.5.cloned.1.call-update) | async-done | bytes 4194320 | tf_op jit(solution)/shard_map/reduce_scatter | solution.py:46
  649.8 3.8 convert_element_type.19
  (17 shorter events, 0.2 us)
Async XLA Ops:
  7.2 13.4 %copy-start.2 = (bf16[1024,512]{1,0:T(8,128)(2,1)S(1)}, bf16[1024,512]{1,0:T(8,128)(2,1)}, u32[]{:S(2)}) copy-start(bf16[1024,512]{1,0:T(8,128)(2,1)} %param.8) | copy-start | bytes 3145732
  7.2 13.4 %copy-start.1 = (bf16[1024,512]{1,0:T(8,128)(2,1)S(1)}, bf16[1024,512]{1,0:T(8,128)(2,1)}, u32[]{:S(2)}) copy-start(bf16[1024,512]{1,0:T(8,128)(2,1)} %param.9) | copy-start | bytes 3145732
  7.2 68.4 %all-reduce.3.cloned.1.call-start = ((), (), s32[]{:S(2)}) async-start(), calls=%async_computation.2 | async-start | bytes 2097152 | tf_op jit(solution)/shard_map/psum | solution.py:18
  23.4 1.0 copy-start.4
  23.4 1.2 copy-start
  23.5 141.6 %all-gather.2.cloned.1.call-start = ((), (), s32[]{:S(2)}) async-start(), calls=%async_computation.4 | async-start | bytes 10485760 | tf_op jit(solution)/shard_map/all_gather | solution.py:42
  24.2 297.8 %reduce-scatter.3.cloned.1.call-start = ((), (), s32[]{:S(2)}) async-start(), calls=%async_computation.3 | async-start | bytes 20971520 | tf_op jit(solution)/shard_map/reduce_scatter | solution.py:32
  90.7 3.5 copy-start.3
  113.6 536.1 %reduce-scatter.5.cloned.1.call-start = ((), (), s32[]{:S(2)}) async-start(), calls=%async_computation.5 | async-start | bytes 37748736 | tf_op jit(solution)/shard_map/reduce_scatter | solution.py:46
Sparse Core Ops, SparseCore 0:
  23.6 51.9 all-reduce.2
  77.4 87.5 all-gather.1
  168.1 153.8 reduce-scatter.2
  324.2 325.5 reduce-scatter.4
where the time goes:
time: 660 us
  waiting for transfers between devices  561 us (85%)
  matrix products  59.3 us (9%)
  between operations  13.9 us (2%)
  blocking collectives  11.4 us (2%)
  other arithmetic  8.36 us (1%)
    reduce_scatter x1, waiting for transfers between devices, local(): lax.psum_scatter(partial_input, 'chan', scatter_dimension=1, tiled=True)  323 us
    reduce_scatter x1, waiting for transfers between devices, local(): lax.psum_scatter(lax.dot_general(hidden_in, grad_z, (((0,), (0,)), ((), (...  139 us
    all_gather x1, waiting for transfers between devices, local(): lax.all_gather(proj_weight, 'dp', axis=0, tiled=True)  51.1 us
    psum x1, waiting for transfers between devices, local(): dmat = lax.psum(local_moment, 'dp')  48 us
    dot_general x1, matrix products, local(): lax.dot_general(grad_z, lax.all_gather(proj_weight, 'dp', axis=0, tiled=T...  18.2 us
    dot_general x1, matrix products, local(): lax.dot_general(hidden_in, grad_z, (((0,), (0,)), ((), ())), preferred_el...  15.7 us
  transfers between devices with their start and end apart: 4, of which 4 were waited for; matrix products, arithmetic and copies ran while one was open for 10% of the time, Pallas kernels for 0%

commit v1 on v0

v1 whole, which is shorter than its diff:
```python
import jax
import jax.numpy as jnp
from jax import lax
from jax.sharding import PartitionSpec as P

F32, BF16 = jnp.float32, jnp.bfloat16
HI = lax.Precision.HIGHEST
MID = lax.Precision.HIGH


def dot(a, b, dims=((1,), (0,)), precision=None):
    return lax.dot_general(a, b, (dims, ((), ())), precision=precision, preferred_element_type=F32)


def pair(x):
    high = x.astype(BF16)
    return high, (x - high.astype(F32)).astype(BF16)


def local(hidden_in, proj_weight, embed, embed_grad, eigvec, eigval):
    rows = embed.shape[0] * lax.axis_size("dp")
    ones = jnp.ones((8, embed.shape[0]), BF16)
    sums_z, sums_g = dot(ones, embed), dot(ones, embed_grad)
    raw = dot(embed, embed_grad, ((0,), (0,)))
    packed = lax.psum(jnp.concatenate([raw, sums_z, sums_g], axis=0), "dp")
    width = raw.shape[0]
    raw = packed[:width]
    mean_z = packed[width : width + 1] / rows
    mean_g = packed[width + 8 : width + 9] / rows
    dmat = raw - rows * mean_z.T * mean_g
    sym = 0.5 * (dmat + dmat.T)
    root = jnp.sqrt(eigval)
    whiten = dot(eigvec / root[None, :], eigvec, ((1,), (1,)), MID)
    loewner = -1.0 / (root[:, None] * root[None, :] * (root[:, None] + root[None, :]))
    half_rot = dot(eigvec, sym, ((0,), (0,)), MID)
    rotated = dot(half_rot, eigvec, precision=MID)
    half_back = dot(eigvec, loewner * rotated, precision=MID)
    dsigma = dot(half_back, eigvec, ((1,), (1,)), MID) * (2.0 / rows)
    w_hi, w_lo = pair(whiten)
    d_hi, d_lo = pair(dsigma)
    shift = dot(mean_g, whiten, precision=HI) + dot(mean_z, dsigma, precision=HI)
    both = jnp.concatenate([embed_grad, embed], axis=1)
    grad_z = dot(both, jnp.concatenate([w_hi, d_hi], axis=0))
    grad_z += dot(both, jnp.concatenate([w_lo, d_lo], axis=0))
    grad_z = (grad_z - shift).astype(BF16)
    core = lax.rem(lax.axis_index("chan"), 2)
    size = lax.axis_size("chan")
    swap = [(k, k ^ 1) for k in range(size)]
    half = proj_weight.shape[0] // 2
    keep = lax.dynamic_slice_in_dim(proj_weight, core * half, half, 0)
    give = lax.dynamic_slice_in_dim(proj_weight, (1 - core) * half, half, 0)
    mate = lax.ppermute(give, "chan", swap)
    weights = jnp.concatenate([keep, mate], axis=1)
    weights = lax.all_gather(weights, "dp", axis=0, tiled=True)
    both_z = jnp.concatenate([grad_z, lax.ppermute(grad_z, "chan", swap)], axis=1)
    partial_input = dot(both_z, weights, ((1,), (1,))).astype(BF16)
    lines = [list(range(c, size, 2)) for c in range(2)]
    grad_hidden = lax.psum_scatter(
        partial_input, "chan", scatter_dimension=1, axis_index_groups=lines, tiled=True
    )
    partial_weight = dot(hidden_in, grad_z, ((0,), (0,))).astype(BF16)
    grad_weight = lax.psum_scatter(partial_weight, "dp", scatter_dimension=0, tiled=True)
    return (grad_weight, grad_hidden)


def solution(mesh):
    in_specs = (
        P("dp", None),
        P("dp", "chan"),
        P("dp", "chan"),
        P("dp", "chan"),
        P("chan", None),
        P("chan"),
    )
    out_specs = (P("dp", "chan"), P("dp", "chan"))
    return jax.shard_map(local, mesh=mesh, in_specs=in_specs, out_specs=out_specs, check_vma=False)
```

time: 660 us -> 403 us (0.61)
  waiting for transfers between devices: 561 us -> 326 us
  matrix products: 59.3 us -> 46.5 us
  blocking collectives: 11.4 us -> 0 us
    reduce_scatter x2, waiting for transfers between devices: 461 us -> 218 us  [the longest x1 143 us: local(): lax.psum_scatter(partial_input, 'chan', scatter_dimension=1, axis_index_g...]
    dot_general x10 -> x14, matrix products: 59.3 us -> 46.5 us  [dot(): lax.dot_general(a, b, (dims, ((), ())), precision=precision, preferred_el...]
    psum x1 -> x0, blocking collectives: 11.4 us -> none  [local(): lax.psum((jnp.sum(zlocal, axis=0), jnp.sum(glocal, axis=0)), 'dp')]
  transfers between devices with their start and end apart: 4 -> 6, of which waited for: 4 -> 6; matrix products, arithmetic and copies ran while one was open for 10% -> 14% of each run, Pallas kernels for 0% -> 0%
where the time goes in v1:
time: 403 us; the launch traced here: 402 us
  waiting for transfers between devices  326 us (81%)
  matrix products  46.5 us (12%)
  between operations  13.9 us (3%)
  local copies, waits for them, and re-layouts  9.31 us (2%)
  other arithmetic  6 us (1%)
    reduce_scatter x1, waiting for transfers between devices, local(): lax.psum_scatter(partial_input, 'chan', scatter_dimension=1, axis_index_g...  143 us
    reduce_scatter x1, waiting for transfers between devices, local(): lax.psum_scatter(partial_weight, 'dp', scatter_dimension=0, tiled=True)  75 us
    all_gather x1, waiting for transfers between devices, local(): weights = lax.all_gather(weights, 'dp', axis=0, tiled=True)  56.3 us
    psum x1, waiting for transfers between devices, local(): packed = lax.psum(jnp.concatenate([raw, sums_z, sums_g], axis=0), 'dp')  47.9 us
    dot_general x14, matrix products, dot(): lax.dot_general(a, b, (dims, ((), ())), precision=precision, preferred_el...  46.5 us
  transfers between devices with their start and end apart: 6, of which 6 were waited for; matrix products, arithmetic and copies ran while one was open for 14% of the time, Pallas kernels for 0%

profile of v1, /device:TPU:0, one launch (start us, length us, event | category | flops | bytes accessed | tf_op | source)
XLA Modules:
  0.0 402.0 jit_solution(11524568279045296995)
XLA Ops:
  7.2 2.8 constant_dynamic-slice_fusion.1
  11.0 0.7 fusion.32
  11.7 1.1 pad_maximum_fusion.1
  13.1 2.8 pad_maximum_fusion
  16.9 1.3 copy-done.4
  18.3 2.4 subtract_convert_fusion.2
  20.6 47.9 %all-reduce.2.cloned.1.call-done = f32[528,512]{1,0:T(8,128)} async-done(((f32[528,512]{1,0:T(8,128)}), f32[528,512]{1,0:T(8,128)}) %all-reduce.2.cloned.1.call-update) | async-done | bytes 1081360 | tf_op jit(solution)/shard_map/psum | solution.py:25
  68.5 0.7 slice_multiply_fusion.1
  69.2 1.4 slice_subtract_fusion
  71.0 1.1 fusion.14
  72.1 1.2 convolution_multiply_fusion.1
  73.2 1.9 fusion.33
  75.1 1.9 subtract_convert_fusion.1
  77.0 1.5 fusion.22
  78.5 1.3 fusion.24
  79.9 1.3 fusion.6
  81.2 1.3 subtract_convert_fusion
  82.5 16.9 %fusion = bf16[8192,512]{0,1:T(8,128)(2,1)} fusion(bf16[1024,512]{0,1:T(8,128)(2,1)S(1)} %subtract_convert_fusion, bf16[1024,8192]{1,0:T(8,128)(2,1)} %param.6), kind=kOutput, calls=%fused_computation.1 | convolution fusion | flops 8594128896 | bytes 26214400 | tf_op jit(solution)/shard_map/dot_general | solution.py:12
  99.6 2.6 collective-permute-done
  102.3 56.3 %all-gather.2.cloned.1.call-done = bf16[4096,1024]{1,0:T(8,128)(2,1)} async-done(((bf16[1024,1024]{1,0:T(8,128)(2,1)}), bf16[4096,1024]{1,0:T(8,128)(2,1)}) %all-gather.2.cloned.1.call-update) | async-done | bytes 8388624 | tf_op jit(solution)/shard_map/all_gather | solution.py:54
  158.6 14.5 %convolution_convert_fusion.1 = bf16[1024,4096]{1,0:T(8,128)(2,1)} fusion(bf16[4096,1024]{1,0:T(8,128)(2,1)} %all-gather.2.cloned.1.call-done, bf16[1024,512]{0,1:T(8,128)(2,1)S(1)} %collective-permute-done, bf16[1024,512]{0,1:T(8,128)(2,1)S(1)} %subtract_convert_fusion), kind=kOutput, calls=%fused_computation.2 | convolution fusion | flops 8598323200 | bytes 18874368 | tf_op jit(solution)/shard_map/dot_general | solution.py:12
  173.1 75.0 %reduce-scatter.3.cloned.1.call-done = bf16[2048,512]{0,1:T(8,128)(2,1)} async-done(((bf16[8192,512]{0,1:T(8,128)(2,1)}), bf16[2048,512]{0,1:T(8,128)(2,1)}) %reduce-scatter.3.cloned.1.call-update) | async-done | bytes 2097168 | tf_op jit(solution)/shard_map/reduce_scatter | solution.py:62
  248.1 3.9 copy.9
  252.0 143.5 %reduce-scatter.5.cloned.1.call-done = bf16[1024,1024]{1,0:T(8,128)(2,1)} async-done(((bf16[1024,4096]{1,0:T(8,128)(2,1)}), bf16[1024,1024]{1,0:T(8,128)(2,1)}) %reduce-scatter.5.cloned.1.call-update) | async-done | bytes 2097168 | tf_op jit(solution)/shard_map/reduce_scatter | solution.py:58
  (36 shorter events, 2.8 us)
Async XLA Ops:
  7.2 61.3 %all-reduce.2.cloned.1.call-start = ((), (), s32[]{:S(2)}) async-start(), calls=%async_computation.2 | async-start | bytes 2162688 | tf_op jit(solution)/shard_map/psum | solution.py:25
  7.2 3.3 copy-start.2
  7.2 3.5 copy-start.1
  10.0 3.1 collective-permute-start.1
  12.8 145.7 %all-gather.2.cloned.1.call-start = ((), (), s32[]{:S(2)}) async-start(), calls=%async_computation.4 | async-start | bytes 10485760 | tf_op jit(solution)/shard_map/all_gather | solution.py:54
  15.9 0.7 copy-start.6
  16.0 232.1 %reduce-scatter.3.cloned.1.call-start = ((), (), s32[]{:S(2)}) async-start(), calls=%async_computation.3 | async-start | bytes 10485760 | tf_op jit(solution)/shard_map/reduce_scatter | solution.py:62
  16.6 1.7 copy-start
  16.9 1.3 copy-start.4
  75.1 3.4 copy-start.3
  75.1 4.7 %copy-start.8 = (bf16[512,512]{1,0:T(8,128)(2,1)S(1)}, bf16[512,512]{1,0:T(8,128)(2,1)}, u32[]{:S(2)}) copy-start(bf16[512,512]{1,0:T(8,128)(2,1)} %get-tuple-element.5) | copy-start | bytes 1572868
  77.0 2.9 copy-start.5
  79.9 1.3 copy-start.7
  99.5 296.0 %reduce-scatter.5.cloned.1.call-start = ((), (), s32[]{:S(2)}) async-start(), calls=%async_computation.5 | async-start | bytes 10485760 | tf_op jit(solution)/shard_map/reduce_scatter | solution.py:58
  99.6 2.7 collective-permute-start
Sparse Core Ops, SparseCore 0:
  12.9 55.5 all-reduce.1
  70.9 87.5 all-gather.1
  161.6 86.4 reduce-scatter.2
  251.0 144.4 reduce-scatter.4

commit v2 on v1

--- a/solution.py
+++ b/solution.py
@@ -1,11 +1,14 @@
 import jax
 import jax.numpy as jnp
 from jax import lax
+from jax.experimental import pallas as pl
+from jax.experimental.pallas import tpu as pltpu
 from jax.sharding import PartitionSpec as P
 
 F32, BF16 = jnp.float32, jnp.bfloat16
 HI = lax.Precision.HIGHEST
 MID = lax.Precision.HIGH
+MESH = pl.DeviceIdType.MESH
 
 
 def dot(a, b, dims=((1,), (0,)), precision=None):
@@ -63,6 +66,359 @@
     return (grad_weight, grad_hidden)
 
 
+def dot3(a, b):
+    a_hi, a_lo = pair(a)
+    b_hi, b_lo = pair(b)
+    return dot(a_hi, b_hi) + (dot(a_hi, b_lo) + dot(a_lo, b_hi))
+
+
+def fused(
+    hid, w4, z_ref, g_ref, u_ref, ev_ref, gw_ref, gh_ref,
+    mom, mom_in, sums, dmat, mats, shift, gz, gzt, wsc, wf, hb,
+    a1s, a1r, a2s, a2r, b1s, b1r, b2s, b2r,
+    mom_ss, mom_rs, sum_ss, sum_rs, dm_ss, dm_rs, w1_ss, w1_rs, w2_ss, w2_rs, wg_ss, wg_rs,
+    rt_ss, rt_rs, lt_ss, lt_rs, sr_ss, sr_rs, sl_ss, sl_rs, red_ss, red_rs, loc,
+):
+    dp, chan = lax.axis_index("dp"), lax.axis_index("chan")
+    px, py = lax.rem(dp, 2), dp // 2
+    xn, yn, dg = 2 * py + (1 - px), 2 * (1 - py) + px, 2 * (1 - py) + (1 - px)
+    zc, core = chan // 2, lax.rem(chan, 2)
+    mate = 2 * zc + (1 - core)
+    tokens, width = z_ref.shape
+    rows = 4 * tokens
+    quarter = width // 4
+    part = wf.shape[1] // 4
+    half = hb.shape[2]
+    last = 3
+
+    def plane(d):
+        return lax.rem(dp + d, 4)
+
+    def line(d):
+        return lax.rem(chan + d, 8)
+
+    def rdma(src, dst, ss, rs, where):
+        return pltpu.make_async_remote_copy(
+            src_ref=src, dst_ref=dst, send_sem=ss, recv_sem=rs, device_id=where, device_id_type=MESH
+        )
+
+    barrier = pltpu.get_barrier_semaphore()
+    for d in range(1, 4):
+        pl.semaphore_signal(barrier, inc=1, device_id={"dp": plane(d)}, device_id_type=MESH)
+    for d in range(1, 8):
+        pl.semaphore_signal(barrier, inc=1, device_id={"chan": line(d)}, device_id_type=MESH)
+
+    order = [(dg, 0), (dg, 1), (xn, 0), (yn, 1), (yn, 0), (xn, 1), (dp, 0), (dp, 1)]
+    slots = hb.shape[0]
+
+    def fetch(n):
+        block, side = order[n]
+        start = pl.multiple_of(block * (2 * half) + side * half, half)
+        return pltpu.make_async_copy(hid.at[:, pl.ds(start, half)], hb.at[n % slots], loc.at[n % slots])
+
+    for n in range(slots):
+        fetch(n).start()
+
+    ones = jnp.ones((8, tokens), BF16)
+    sums[dp, 0:8, :] = dot(ones, z_ref[...])
+    sums[dp, 8:16, :] = dot(ones, g_ref[...])
+    z_t = z_ref[...].astype(F32).T.astype(BF16)
+    mom[...] = dot(z_t, g_ref[...])
+
+    pl.semaphore_wait(barrier, 10)
+    sends = []
+
+    def go(copy):
+        copy.start()
+        sends.append(copy)
+        return copy
+
+    mom_c, sum_c, w1_c = [], [], []
+    for d in range(1, 4):
+        to = plane(d)
+        where = {"dp": to}
+        start = pl.multiple_of(to * quarter, quarter)
+        mom_c.append(go(rdma(mom.at[pl.ds(start, quarter)], mom_in.at[d], mom_ss.at[d], mom_rs.at[d], where)))
+        sum_c.append(go(rdma(sums.at[dp], sums.at[dp], sum_ss.at[d], sum_rs.at[d], where)))
+    for d in range(1, 4):
+        to = plane(d)
+        w1_c.append(go(rdma(w4.at[:, to], wsc.at[dp], w1_ss.at[d], w1_rs.at[d], {"dp": to})))
+    own_w = pltpu.make_async_copy(w4.at[:, dp], wsc.at[dp], loc.at[slots])
+    own_w.start()
+
+    u = u_ref[...]
+    root_row = jnp.broadcast_to(jnp.sqrt(ev_ref[...]), (width, width))
+    u_t = u.T
+    whiten = dot3(u / root_row, u_t)
+    mats[0], mats[1] = pair(whiten)
+    root_col = root_row.T
+    loewner = -1.0 / (root_row * root_col * (root_row + root_col))
+
+    for c in mom_c:
+        c.wait_recv()
+    mine = pl.ds(pl.multiple_of(dp * quarter, quarter), quarter)
+    dmat[mine, :] = (mom[mine, :] + mom_in[1]) + (mom_in[2] + mom_in[3])
+    dm_c = []
+    for d in range(1, 4):
+        dm_c.append(go(rdma(dmat.at[mine], dmat.at[mine], dm_ss.at[d], dm_rs.at[d], {"dp": plane(d)})))
+    for c in sum_c:
+        c.wait_recv()
+    for c in w1_c:
+        c.wait_recv()
+    own_w.wait()
+    my_part = pl.ds(pl.multiple_of(dp * part, part), part)
+    w2_c = []
+    for d in range(1, 8):
+        to = line(d)
+        w2_c.append(
+            go(
+                rdma(
+                    wsc.at[to // 2, lax.rem(to, 2)], wf.at[chan, my_part],
+                    w2_ss.at[d], w2_rs.at[d], {"chan": to},
+                )
+            )
+        )
+    own_w2 = pltpu.make_async_copy(wsc.at[zc, core], wf.at[chan, my_part], loc.at[slots])
+    own_w2.start()
+    for c in dm_c:
+        c.wait_recv()
+
+    total = (sums[0] + sums[1]) + (sums[2] + sums[3])
+    mean_z, mean_g = total[0:8] / rows, total[8:16] / rows
+    col_z = jnp.broadcast_to(mean_z[0:1], (width, width)).T
+    raw = dmat[...] - rows * col_z * mean_g[0:1]
+    sym = 0.5 * (raw + raw.T)
+    rotated = dot3(dot3(u_t, sym), u)
+    dsigma = dot3(dot3(u, loewner * rotated), u_t) * (2.0 / rows)
+    mats[2], mats[3] = pair(dsigma)
+    shift[...] = dot3(mean_g, whiten) + dot3(mean_z, dsigma)
+
+    tile = tokens // 4
+
+    @pl.loop(0, 4)
+    def _(t):
+        here = pl.ds(pl.multiple_of(t * tile, tile), tile)
+        g, z = g_ref[here, :], z_ref[here, :]
+        acc = (dot(g, mats[0]) + dot(z, mats[2])) + (dot(g, mats[1]) + dot(z, mats[3]))
+        acc = acc - shift[0:1, :]
+        gz[chan, here, :] = acc.astype(BF16)
+        gzt[:, here] = acc.T.astype(BF16)
+
+    def moves_right(k):
+        slot = 2 * (zc - k) + core
+        return rdma(gz.at[slot], gz.at[slot], rt_ss.at[k], rt_rs.at[k], {"chan": chan + 2})
+
+    def moves_left(k):
+        slot = 2 * (zc + k) + core
+        return rdma(gz.at[slot], gz.at[slot], lt_ss.at[k], lt_rs.at[k], {"chan": chan - 2})
+
+    def from_left(k):
+        slot = 2 * (zc - 1 - k) + core
+        return rdma(gz.at[slot], gz.at[slot], rt_ss.at[k], rt_rs.at[k], {"chan": chan - 2})
+
+    def from_right(k):
+        slot = 2 * (zc + 1 + k) + core
+        return rdma(gz.at[slot], gz.at[slot], lt_ss.at[k], lt_rs.at[k], {"chan": chan + 2})
+
+    def to_mate(block, ss, rs):
+        slot = 2 * block + core
+        return rdma(gz.at[slot], gz.at[slot], ss, rs, {"chan": mate})
+
+    def has_left(k):
+        return zc - 1 - k >= 0
+
+    def has_right(k):
+        return zc + 1 + k <= last
+
+    def sends_right(k):
+        return jnp.logical_and(zc - k >= 0, zc < last)
+
+    def sends_left(k):
+        return jnp.logical_and(zc + k <= last, zc > 0)
+
+    def push(k):
+        pl.when(sends_right(k))(lambda: moves_right(k).start())
+        pl.when(sends_left(k))(lambda: moves_left(k).start())
+
+    def take(k):
+        @pl.when(has_left(k))
+        def _():
+            from_left(k).wait_recv()
+            if k < 2:
+                pl.when(zc < last)(lambda: moves_right(k + 1).start())
+            to_mate(zc - 1 - k, sr_ss.at[k], sr_rs.at[k]).start()
+
+        @pl.when(has_right(k))
+        def _():
+            from_right(k).wait_recv()
+            if k < 2:
+                pl.when(zc > 0)(lambda: moves_left(k + 1).start())
+            to_mate(zc + 1 + k, sl_ss.at[k], sl_rs.at[k]).start()
+
+    push(0)
+    own_mate = go(to_mate(zc, sr_ss.at[3], sr_rs.at[3]))
+
+    cols = half // 4
+
+    def product(n, emit):
+        fetch(n).wait()
+
+        @pl.loop(0, 4)
+        def _(t):
+            here = pl.ds(pl.multiple_of(t * cols, cols), cols)
+            emit(here, dot(gzt[...], hb[n % slots, :, here]))
+
+        if n + slots < len(order):
+            fetch(n + slots).start()
+
+    def store(dst, idx):
+        def emit(here, value):
+            dst[idx, :, here] = value.astype(BF16)
+
+        return emit
+
+    to_x, to_y = {"dp": xn}, {"dp": yn}
+    product(0, store(a1s, 1))
+    a1_dg = go(rdma(a1s.at[1], a1r.at[1], red_ss.at[0], red_rs.at[0], to_x))
+    product(1, store(b1s, 1))
+    b1_dg = go(rdma(b1s.at[1], b1r.at[1], red_ss.at[1], red_rs.at[1], to_y))
+    product(2, store(a1s, 0))
+    a1_own = go(rdma(a1s.at[0], a1r.at[0], red_ss.at[2], red_rs.at[2], to_x))
+    product(3, store(b1s, 0))
+    b1_own = go(rdma(b1s.at[0], b1r.at[0], red_ss.at[3], red_rs.at[3], to_y))
+
+    take(0)
+    for c in w2_c:
+        c.wait_recv()
+    own_w2.wait()
+    wg_x = go(rdma(wf.at[:, my_part], wf.at[:, my_part], wg_ss.at[0], wg_rs.at[0], to_x))
+    wg_y = go(rdma(wf.at[:, my_part], wf.at[:, my_part], wg_ss.at[1], wg_rs.at[1], to_y))
+
+    def store_sum(dst, more):
+        def emit(here, value):
+            dst[:, here] = (value + more[1, :, here].astype(F32)).astype(BF16)
+
+        return emit
+
+    a1_dg.wait_recv()
+    product(4, store_sum(a2s, a1r))
+    a2 = go(rdma(a2s, a2r, red_ss.at[4], red_rs.at[4], to_y))
+    b1_dg.wait_recv()
+    product(5, store_sum(b2s, b1r))
+    b2 = go(rdma(b2s, b2r, red_ss.at[5], red_rs.at[5], to_x))
+
+    take(1)
+    half_part = part // 2
+    wg_y.wait_recv()
+    first = pl.ds(pl.multiple_of(yn * part, part), half_part)
+    relay_x = go(rdma(wf.at[:, first], wf.at[:, first], wg_ss.at[2], wg_rs.at[2], to_x))
+    wg_x.wait_recv()
+    second = pl.ds(pl.multiple_of(xn * part + half_part, half_part), half_part)
+    relay_y = go(rdma(wf.at[:, second], wf.at[:, second], wg_ss.at[3], wg_rs.at[3], to_y))
+    take(2)
+
+    own_mate.wait_recv()
+    for k in range(3):
+        pl.when(has_left(k))(lambda k=k: to_mate(zc - 1 - k, sr_ss.at[k], sr_rs.at[k]).wait_recv())
+        pl.when(has_right(k))(lambda k=k: to_mate(zc + 1 + k, sl_ss.at[k], sl_rs.at[k]).wait_recv())
+
+    def hidden_part(owner):
+        these = pl.ds(pl.multiple_of(owner * part, part), part)
+        block = tokens // 2
+
+        @pl.loop(0, 2)
+        def _(t):
+            here = pl.ds(pl.multiple_of(t * block, block), block)
+            acc = dot(gz[0, here, :], wf[0, these, :], ((1,), (1,)))
+            for e in range(1, 8):
+                acc += dot(gz[e, here, :], wf[e, these, :], ((1,), (1,)))
+            gh_ref[here, these] = acc.astype(BF16)
+
+    hidden_part(dp)
+    hidden_part(xn)
+    hidden_part(yn)
+
+    def finish(side, first_in, second_in):
+        def emit(here, value):
+            value = value + first_in[0, :, here].astype(F32) + second_in[:, here].astype(F32)
+            to = pl.ds(pl.multiple_of(side * half + here.start, cols), cols)
+            gw_ref[to, :] = value.T.astype(BF16)
+
+        return emit
+
+    a1_own.wait_recv()
+    a2.wait_recv()
+    product(6, finish(0, a1r, a2r))
+    b1_own.wait_recv()
+    b2.wait_recv()
+    product(7, finish(1, b1r, b2r))
+    relay_x.wait_recv()
+    relay_y.wait_recv()
+    hidden_part(dg)
+
+    for c in sends:
+        c.wait_send()
+    for k in range(3):
+        pl.when(sends_right(k))(lambda k=k: moves_right(k).wait_send())
+        pl.when(sends_left(k))(lambda k=k: moves_left(k).wait_send())
+        pl.when(has_left(k))(lambda k=k: to_mate(zc - 1 - k, sr_ss.at[k], sr_rs.at[k]).wait_send())
+        pl.when(has_right(k))(lambda k=k: to_mate(zc + 1 + k, sl_ss.at[k], sl_rs.at[k]).wait_send())
+
+
+def local_fused(hidden_in, proj_weight, embed, embed_grad, eigvec, eigval):
+    tokens, width = embed.shape
+    feats = proj_weight.shape[0]
+    part, half = feats // 8, feats // 2
+    vmem, anyspace = pl.BlockSpec(memory_space=pltpu.VMEM), pl.BlockSpec(memory_space=pl.ANY)
+    dma = pltpu.SemaphoreType.DMA
+    slots = 4
+    return pl.pallas_call(
+        fused,
+        out_shape=(
+            jax.ShapeDtypeStruct((feats, width), BF16),
+            jax.ShapeDtypeStruct((tokens, half), BF16),
+        ),
+        in_specs=[anyspace, anyspace, vmem, vmem, vmem, vmem],
+        out_specs=(vmem, vmem),
+        scratch_shapes=[
+            pltpu.VMEM((width, width), F32),
+            pltpu.VMEM((4, width // 4, width), F32),
+            pltpu.VMEM((4, 16, width), F32),
+            pltpu.VMEM((width, width), F32),
+            pltpu.VMEM((4, width, width), BF16),
+            pltpu.VMEM((8, width), F32),
+            pltpu.VMEM((8, tokens, width), BF16),
+            pltpu.VMEM((width, tokens), BF16),
+            pltpu.VMEM((4, 2, part, width), BF16),
+            pltpu.VMEM((8, half, width), BF16),
+            pltpu.VMEM((slots, tokens, half), BF16),
+        ]
+        + [
+            pltpu.VMEM((2, width, half), BF16),
+            pltpu.VMEM((2, width, half), BF16),
+            pltpu.VMEM((width, half), BF16),
+            pltpu.VMEM((width, half), BF16),
+        ]
+        * 2
+        + [dma((4,))] * 8
+        + [dma((8,))] * 2
+        + [dma((4,))] * 10
+        + [dma((6,))] * 2
+        + [dma((slots + 1,))],
+        compiler_params=pltpu.CompilerParams(
+            collective_id=0, has_side_effects=True, vmem_limit_bytes=63 * 2**20
+        ),
+        cost_estimate=pl.CostEstimate(flops=20 * 10**9, bytes_accessed=30 * 10**6, transcendentals=0),
+    )(
+        hidden_in,
+        proj_weight.reshape(2, 4, part, width),
+        embed,
+        embed_grad,
+        eigvec,
+        eigval.reshape(1, width),
+    )
+
+
 def solution(mesh):
     in_specs = (
         P("dp", None),
@@ -73,4 +429,6 @@
         P("chan"),
     )
     out_specs = (P("dp", "chan"), P("dp", "chan"))
-    return jax.shard_map(local, mesh=mesh, in_specs=in_specs, out_specs=out_specs, check_vma=False)
+    small = mesh.shape["dp"] == 4 and mesh.shape["chan"] == 8
+    run = local_fused if small else local
+    return jax.shard_map(run, mesh=mesh, in_specs=in_specs, out_specs=out_specs, check_vma=False)

time: 403 us -> 215 us (0.53)
  waiting for transfers between devices: 326 us -> 0 us
  Pallas kernels: 0 us -> 209 us
  matrix products: 46.5 us -> 0 us
  between operations: 13.9 us -> 0.65 us
  other arithmetic: 6 us -> 0 us
  local copies, waits for them, and re-layouts: 9.31 us -> 4.52 us
    reduce_scatter x2 -> x0, waiting for transfers between devices: 218 us -> none  [the longest x1 143 us: local(): lax.psum_scatter(partial_input, 'chan', scatter_dimension=1, axis_index_g...]
    pallas_call x0 -> x1, Pallas kernels: none -> 209 us  [local_fused(): pl.pallas_call(fused, out_shape=(jax.ShapeDtypeStruct((feats, width), BF1...]
    all_gather x1 -> x0, waiting for transfers between devices: 56.3 us -> none  [local(): weights = lax.all_gather(weights, 'dp', axis=0, tiled=True)]
    psum x1 -> x0, waiting for transfers between devices: 47.9 us -> none  [local(): packed = lax.psum(jnp.concatenate([raw, sums_z, sums_g], axis=0), 'dp')]
    dot_general x14 -> x0, matrix products: 46.5 us -> none  [dot(): lax.dot_general(a, b, (dims, ((), ())), precision=precision, preferred_el...]
  transfers between devices with their start and end apart: 6 -> 0, of which waited for: 6 -> 0; matrix products, arithmetic and copies ran while one was open for 14% -> 0% of each run, Pallas kernels for 0% -> 0%
where the time goes in v2:
time: 215 us; the launch traced here: 214 us
  Pallas kernels  209 us (97%)
  local copies, waits for them, and re-layouts  4.52 us (2%)
    pallas_call x1, Pallas kernels, local_fused(): pl.pallas_call(fused, out_shape=(jax.ShapeDtypeStruct((feats, width), BF1...  209 us
    unnamed x4, local copies, waits for them, and re-layouts  4.52 us

profile of v2, /device:TPU:0, one launch (start us, length us, event | category | flops | bytes accessed | tf_op | source)
XLA Modules:
  0.0 214.4 jit_solution(3803769983288370268)
XLA Ops:
  0.6 209.2 %shard_map.77 = (bf16[2048,512]{1,0:T(8,128)(2,1)}, bf16[1024,1024]{1,0:T(8,128)(2,1)}) custom-call(bf16[1024,8192]{1,0:T(8,128)(2,1)} %hid.1, bf16[2,4,256,512]{3,2,1,0:T(8,128)(2,1)} %bitcast.2, bf16[1024,512]{1,0:T(8,128)(2,1)} %z_ref.1, bf16[1024,512]{1,0:T(8,128)(2,1)} %g_ref.1, f32[512,512]{1,0:T(8,128)} %u_ref.1, f32[1,512]{1,0:T(1,128)} %bitcast.3), custom_call_target="tpu_custom_call" | custom-call | flops 20000000000 | bytes 30000000 | tf_op jit(solution)/shard_map/pallas_call | solution.py:375
  209.8 0.0 copy-start
  209.8 3.2 %copy.10 = bf16[2048,512]{1,0:T(8,128)(2,1)} copy(bf16[2048,512]{1,0:T(8,128)(2,1)} %get-tuple-element.4) | data formatting | bytes 4194304
  213.0 0.0 copy-done
  213.0 1.3 copy.11
Async XLA Ops:
  209.8 3.2 %copy-start = (bf16[1024,1024]{1,0:T(8,128)(2,1)S(1)}, bf16[1024,1024]{1,0:T(8,128)(2,1)}, u32[]{:S(2)}) copy-start(bf16[1024,1024]{1,0:T(8,128)(2,1)} %get-tuple-element.5) | copy-start | bytes 6291460

commit v3 on v2

--- a/solution.py
+++ b/solution.py
@@ -74,7 +74,7 @@
 
 def fused(
     hid, w4, z_ref, g_ref, u_ref, ev_ref, gw_ref, gh_ref,
-    mom, mom_in, sums, dmat, mats, shift, gz, gzt, wsc, wf, hb,
+    mom, mom_in, sums, dmat, mats, shift, acc_t, gz, gzt, wsc, wf, hb,
     a1s, a1r, a2s, a2r, b1s, b1r, b2s, b2r,
     mom_ss, mom_rs, sum_ss, sum_rs, dm_ss, dm_rs, w1_ss, w1_rs, w2_ss, w2_rs, wg_ss, wg_rs,
     rt_ss, rt_rs, lt_ss, lt_rs, sr_ss, sr_rs, sl_ss, sl_rs, red_ss, red_rs, loc,
@@ -174,12 +174,46 @@
             go(
                 rdma(
                     wsc.at[to // 2, lax.rem(to, 2)], wf.at[chan, my_part],
-                    w2_ss.at[d], w2_rs.at[d], {"chan": to},
+                    w2_ss.at[d], w2_rs.at[chan], {"chan": to},
                 )
             )
         )
     own_w2 = pltpu.make_async_copy(wsc.at[zc, core], wf.at[chan, my_part], loc.at[slots])
     own_w2.start()
+
+    to_x, to_y = {"dp": xn}, {"dp": yn}
+    half_part = part // 2
+
+    def landed(source):
+        ref = wf.at[source, my_part]
+        rdma(ref, ref, w2_ss.at[0], w2_rs.at[source], {"chan": mate}).wait_recv()
+
+    def group(k):
+        return pl.ds(2 * lax.rem(zc + k, 4), 2)
+
+    def spread(k):
+        ref = wf.at[group(k), my_part]
+        wg_c.append(
+            [
+                go(rdma(ref, ref, wg_ss.at[4 * n + k], wg_rs.at[4 * n + k], where))
+                for n, where in enumerate((to_x, to_y))
+            ]
+        )
+
+    def relay(k):
+        ways = (
+            (2, wg_c[k][1], yn * part, to_x),
+            (3, wg_c[k][0], xn * part + half_part, to_y),
+        )
+        for n, arrived, start, where in ways:
+            arrived.wait_recv()
+            ref = wf.at[group(k), pl.ds(pl.multiple_of(start, half_part), half_part)]
+            relay_c.append(go(rdma(ref, ref, wg_ss.at[4 * n + k], wg_rs.at[4 * n + k], where)))
+
+    wg_c, relay_c = [], []
+    own_w2.wait()
+    landed(mate)
+    spread(0)
     for c in dm_c:
         c.wait_recv()
 
@@ -277,22 +311,25 @@
 
         return emit
 
-    to_x, to_y = {"dp": xn}, {"dp": yn}
     product(0, store(a1s, 1))
     a1_dg = go(rdma(a1s.at[1], a1r.at[1], red_ss.at[0], red_rs.at[0], to_x))
     product(1, store(b1s, 1))
     b1_dg = go(rdma(b1s.at[1], b1r.at[1], red_ss.at[1], red_rs.at[1], to_y))
+
+    def next_group(k):
+        for c in range(2):
+            landed(2 * lax.rem(zc + k, 4) + c)
+        spread(k)
+
+    next_group(1)
+    relay(0)
     product(2, store(a1s, 0))
     a1_own = go(rdma(a1s.at[0], a1r.at[0], red_ss.at[2], red_rs.at[2], to_x))
     product(3, store(b1s, 0))
     b1_own = go(rdma(b1s.at[0], b1r.at[0], red_ss.at[3], red_rs.at[3], to_y))
-
     take(0)
-    for c in w2_c:
-        c.wait_recv()
-    own_w2.wait()
-    wg_x = go(rdma(wf.at[:, my_part], wf.at[:, my_part], wg_ss.at[0], wg_rs.at[0], to_x))
-    wg_y = go(rdma(wf.at[:, my_part], wf.at[:, my_part], wg_ss.at[1], wg_rs.at[1], to_y))
+    next_group(2)
+    next_group(3)
 
     def store_sum(dst, more):
         def emit(here, value):
@@ -306,15 +343,21 @@
     b1_dg.wait_recv()
     product(5, store_sum(b2s, b1r))
     b2 = go(rdma(b2s, b2r, red_ss.at[5], red_rs.at[5], to_x))
-
+    relay(1)
     take(1)
-    half_part = part // 2
-    wg_y.wait_recv()
-    first = pl.ds(pl.multiple_of(yn * part, part), half_part)
-    relay_x = go(rdma(wf.at[:, first], wf.at[:, first], wg_ss.at[2], wg_rs.at[2], to_x))
-    wg_x.wait_recv()
-    second = pl.ds(pl.multiple_of(xn * part + half_part, half_part), half_part)
-    relay_y = go(rdma(wf.at[:, second], wf.at[:, second], wg_ss.at[3], wg_rs.at[3], to_y))
+
+    def keep(side, first_in):
+        def emit(here, value):
+            acc_t[side, :, here] = value + first_in[0, :, here].astype(F32)
+
+        return emit
+
+    relay(2)
+    a1_own.wait_recv()
+    product(6, keep(0, a1r))
+    b1_own.wait_recv()
+    product(7, keep(1, b1r))
+    relay(3)
     take(2)
 
     own_mate.wait_recv()
@@ -338,22 +381,18 @@
     hidden_part(xn)
     hidden_part(yn)
 
-    def finish(side, first_in, second_in):
-        def emit(here, value):
-            value = value + first_in[0, :, here].astype(F32) + second_in[:, here].astype(F32)
-            to = pl.ds(pl.multiple_of(side * half + here.start, cols), cols)
-            gw_ref[to, :] = value.T.astype(BF16)
-
-        return emit
-
-    a1_own.wait_recv()
-    a2.wait_recv()
-    product(6, finish(0, a1r, a2r))
-    b1_own.wait_recv()
-    b2.wait_recv()
-    product(7, finish(1, b1r, b2r))
-    relay_x.wait_recv()
-    relay_y.wait_recv()
+    for side, arrived, ref in ((0, a2, a2r), (1, b2, b2r)):
+        arrived.wait_recv()
+
+        @pl.loop(0, 4)
+        def _(t):
+            start = pl.multiple_of(t * cols, cols)
+            here = pl.ds(start, cols)
+            value = acc_t[side, :, here] + ref[:, here].astype(F32)
+            gw_ref[pl.ds(pl.multiple_of(side * half + start, cols), cols), :] = value.T.astype(BF16)
+
+    for c in relay_c:
+        c.wait_recv()
     hidden_part(dg)
 
     for c in sends:
@@ -387,6 +426,7 @@
             pltpu.VMEM((width, width), F32),
             pltpu.VMEM((4, width, width), BF16),
             pltpu.VMEM((8, width), F32),
+            pltpu.VMEM((2, width, half), F32),
             pltpu.VMEM((8, tokens, width), BF16),
             pltpu.VMEM((width, tokens), BF16),
             pltpu.VMEM((4, 2, part, width), BF16),
@@ -402,7 +442,8 @@
         * 2
         + [dma((4,))] * 8
         + [dma((8,))] * 2
-        + [dma((4,))] * 10
+        + [dma((16,))] * 2
+        + [dma((4,))] * 8
         + [dma((6,))] * 2
         + [dma((slots + 1,))],
         compiler_params=pltpu.CompilerParams(

time: 215 us -> 204 us (0.949)
  Pallas kernels: 209 us -> 198 us
    pallas_call x1, Pallas kernels: 209 us -> 198 us  [local_fused(): pl.pallas_call(fused, out_shape=(jax.ShapeDtypeStruct((feats, width), BF1...]
where the time goes in v3:
time: 204 us; the launch traced here: 203 us
  Pallas kernels  198 us (97%)
  local copies, waits for them, and re-layouts  4.52 us (2%)
    pallas_call x1, Pallas kernels, local_fused(): pl.pallas_call(fused, out_shape=(jax.ShapeDtypeStruct((feats, width), BF1...  198 us
    unnamed x4, local copies, waits for them, and re-layouts  4.52 us

profile of v3, /device:TPU:0, one launch (start us, length us, event | category | flops | bytes accessed | tf_op | source)
XLA Modules:
  0.0 203.4 jit_solution(523142686045428121)
XLA Ops:
  0.6 198.2 %shard_map.77 = (bf16[2048,512]{1,0:T(8,128)(2,1)}, bf16[1024,1024]{1,0:T(8,128)(2,1)}) custom-call(bf16[1024,8192]{1,0:T(8,128)(2,1)} %hid.1, bf16[2,4,256,512]{3,2,1,0:T(8,128)(2,1)} %bitcast.2, bf16[1024,512]{1,0:T(8,128)(2,1)} %z_ref.1, bf16[1024,512]{1,0:T(8,128)(2,1)} %g_ref.1, f32[512,512]{1,0:T(8,128)} %u_ref.1, f32[1,512]{1,0:T(1,128)} %bitcast.3), custom_call_target="tpu_custom_call" | custom-call | flops 20000000000 | bytes 30000000 | tf_op jit(solution)/shard_map/pallas_call | solution.py:414
  198.8 0.0 copy-start
  198.8 3.2 %copy.10 = bf16[2048,512]{1,0:T(8,128)(2,1)} copy(bf16[2048,512]{1,0:T(8,128)(2,1)} %get-tuple-element.4) | data formatting | bytes 4194304
  202.0 0.0 copy-done
  202.0 1.3 copy.11
Async XLA Ops:
  198.8 3.2 %copy-start = (bf16[1024,1024]{1,0:T(8,128)(2,1)S(1)}, bf16[1024,1024]{1,0:T(8,128)(2,1)}, u32[]{:S(2)}) copy-start(bf16[1024,1024]{1,0:T(8,128)(2,1)} %get-tuple-element.5) | copy-start | bytes 6291460

commit v4 on v3

--- a/solution.py
+++ b/solution.py
@@ -74,7 +74,7 @@
 
 def fused(
     hid, w4, z_ref, g_ref, u_ref, ev_ref, gw_ref, gh_ref,
-    mom, mom_in, sums, dmat, mats, shift, acc_t, gz, gzt, wsc, wf, hb,
+    mom, mom_in, sums, dmat, sym_ref, mats, shift, acc_t, gz, gzt, wsc, wf, hb,
     a1s, a1r, a2s, a2r, b1s, b1r, b2s, b2r,
     mom_ss, mom_rs, sum_ss, sum_rs, dm_ss, dm_rs, w1_ss, w1_rs, w2_ss, w2_rs, wg_ss, wg_rs,
     rt_ss, rt_rs, lt_ss, lt_rs, sr_ss, sr_rs, sl_ss, sl_rs, red_ss, red_rs, loc,
@@ -123,7 +123,17 @@
     sums[dp, 0:8, :] = dot(ones, z_ref[...])
     sums[dp, 8:16, :] = dot(ones, g_ref[...])
     z_t = z_ref[...].astype(F32).T.astype(BF16)
-    mom[...] = dot(z_t, g_ref[...])
+    raw = dot(z_t, g_ref[...])
+    raw = 0.5 * (raw + raw.T)
+    mid = width // 2
+    row_at = lax.broadcasted_iota(jnp.int32, (mid, mid), 0)
+    col_at = lax.broadcasted_iota(jnp.int32, (mid, mid), 1)
+    top = raw[:mid, :mid]
+    diag = jnp.sum(jnp.where(row_at == col_at, top, 0.0), axis=0, keepdims=True)
+    sums[dp, 16:24, :mid] = jnp.broadcast_to(diag, (8, mid))
+    sums[dp, 16:24, mid:] = jnp.zeros((8, mid), F32)
+    mom[:mid, :] = raw[:mid, mid:]
+    mom[mid:, :] = jnp.where(row_at < col_at, top, raw[mid:, mid:])
 
     pl.semaphore_wait(barrier, 10)
     sends = []
@@ -188,8 +198,10 @@
         ref = wf.at[source, my_part]
         rdma(ref, ref, w2_ss.at[0], w2_rs.at[source], {"chan": mate}).wait_recv()
 
+    paired = (zc, zc + 1 - 2 * lax.rem(zc, 2), lax.rem(zc + 2, 4), last - zc)
+
     def group(k):
-        return pl.ds(2 * lax.rem(zc + k, 4), 2)
+        return pl.ds(2 * paired[k], 2)
 
     def spread(k):
         ref = wf.at[group(k), my_part]
@@ -219,9 +231,17 @@
 
     total = (sums[0] + sums[1]) + (sums[2] + sums[3])
     mean_z, mean_g = total[0:8] / rows, total[8:16] / rows
-    col_z = jnp.broadcast_to(mean_z[0:1], (width, width)).T
-    raw = dmat[...] - rows * col_z * mean_g[0:1]
-    sym = 0.5 * (raw + raw.T)
+    cross, packed = dmat[:mid, :], dmat[mid:, :]
+    flipped = packed.T
+    diag = jnp.broadcast_to(total[16:17, :mid], (mid, mid))
+    sym_ref[:mid, :mid] = jnp.where(
+        row_at < col_at, packed, jnp.where(row_at == col_at, diag, flipped)
+    )
+    sym_ref[mid:, mid:] = jnp.where(row_at < col_at, flipped, packed)
+    sym_ref[:mid, mid:] = cross
+    sym_ref[mid:, :mid] = cross.T
+    outer = jnp.broadcast_to(mean_z[0:1], (width, width)).T * mean_g[0:1]
+    sym = sym_ref[...] - (0.5 * rows) * (outer + outer.T)
     rotated = dot3(dot3(u_t, sym), u)
     dsigma = dot3(dot3(u, loewner * rotated), u_t) * (2.0 / rows)
     mats[2], mats[3] = pair(dsigma)
@@ -318,18 +338,15 @@
 
     def next_group(k):
         for c in range(2):
-            landed(2 * lax.rem(zc + k, 4) + c)
+            landed(2 * paired[k] + c)
         spread(k)
 
-    next_group(1)
-    relay(0)
     product(2, store(a1s, 0))
     a1_own = go(rdma(a1s.at[0], a1r.at[0], red_ss.at[2], red_rs.at[2], to_x))
     product(3, store(b1s, 0))
     b1_own = go(rdma(b1s.at[0], b1r.at[0], red_ss.at[3], red_rs.at[3], to_y))
+    relay(0)
     take(0)
-    next_group(2)
-    next_group(3)
 
     def store_sum(dst, more):
         def emit(here, value):
@@ -343,6 +360,9 @@
     b1_dg.wait_recv()
     product(5, store_sum(b2s, b1r))
     b2 = go(rdma(b2s, b2r, red_ss.at[5], red_rs.at[5], to_x))
+    next_group(1)
+    next_group(2)
+    next_group(3)
     relay(1)
     take(1)
 
@@ -420,9 +440,10 @@
         in_specs=[anyspace, anyspace, vmem, vmem, vmem, vmem],
         out_specs=(vmem, vmem),
         scratch_shapes=[
-            pltpu.VMEM((width, width), F32),
-            pltpu.VMEM((4, width // 4, width), F32),
-            pltpu.VMEM((4, 16, width), F32),
+            pltpu.VMEM((width, width // 2), F32),
+            pltpu.VMEM((4, width // 4, width // 2), F32),
+            pltpu.VMEM((4, 24, width), F32),
+            pltpu.VMEM((width, width // 2), F32),
             pltpu.VMEM((width, width), F32),
             pltpu.VMEM((4, width, width), BF16),
             pltpu.VMEM((8, width), F32),

time: 204 us -> 196 us (0.961); the launches traced: 203 us -> 193 us
  Pallas kernels: 198 us -> 188 us
    pallas_call x1, Pallas kernels: 198 us -> 188 us  [local_fused(): pl.pallas_call(fused, out_shape=(jax.ShapeDtypeStruct((feats, width), BF1...]
where the time goes in v4:
time: 196 us; the launch traced here: 193 us
  Pallas kernels  188 us (96%)
  local copies, waits for them, and re-layouts  4.52 us (2%)
    pallas_call x1, Pallas kernels, local_fused(): pl.pallas_call(fused, out_shape=(jax.ShapeDtypeStruct((feats, width), BF1...  188 us
    unnamed x4, local copies, waits for them, and re-layouts  4.52 us

profile of v4, /device:TPU:0, one launch (start us, length us, event | category | flops | bytes accessed | tf_op | source)
XLA Modules:
  0.0 192.9 jit_solution(839396824053914252)
XLA Ops:
  0.6 187.8 %shard_map.77 = (bf16[2048,512]{1,0:T(8,128)(2,1)}, bf16[1024,1024]{1,0:T(8,128)(2,1)}) custom-call(bf16[1024,8192]{1,0:T(8,128)(2,1)} %hid.1, bf16[2,4,256,512]{3,2,1,0:T(8,128)(2,1)} %bitcast.2, bf16[1024,512]{1,0:T(8,128)(2,1)} %z_ref.1, bf16[1024,512]{1,0:T(8,128)(2,1)} %g_ref.1, f32[512,512]{1,0:T(8,128)} %u_ref.1, f32[1,512]{1,0:T(1,128)} %bitcast.3), custom_call_target="tpu_custom_call" | custom-call | flops 20000000000 | bytes 30000000 | tf_op jit(solution)/shard_map/pallas_call | solution.py:434
  188.4 0.0 copy-start
  188.4 3.2 %copy.10 = bf16[2048,512]{1,0:T(8,128)(2,1)} copy(bf16[2048,512]{1,0:T(8,128)(2,1)} %get-tuple-element.4) | data formatting | bytes 4194304
  191.6 0.0 copy-done
  191.6 1.3 copy.11
Async XLA Ops:
  188.4 3.2 %copy-start = (bf16[1024,1024]{1,0:T(8,128)(2,1)S(1)}, bf16[1024,1024]{1,0:T(8,128)(2,1)}, u32[]{:S(2)}) copy-start(bf16[1024,1024]{1,0:T(8,128)(2,1)} %get-tuple-element.5) | copy-start | bytes 6291460

commit v5 on v4

--- a/solution.py
+++ b/solution.py
@@ -150,12 +150,6 @@
         start = pl.multiple_of(to * quarter, quarter)
         mom_c.append(go(rdma(mom.at[pl.ds(start, quarter)], mom_in.at[d], mom_ss.at[d], mom_rs.at[d], where)))
         sum_c.append(go(rdma(sums.at[dp], sums.at[dp], sum_ss.at[d], sum_rs.at[d], where)))
-    for d in range(1, 4):
-        to = plane(d)
-        w1_c.append(go(rdma(w4.at[:, to], wsc.at[dp], w1_ss.at[d], w1_rs.at[d], {"dp": to})))
-    own_w = pltpu.make_async_copy(w4.at[:, dp], wsc.at[dp], loc.at[slots])
-    own_w.start()
-
     u = u_ref[...]
     root_row = jnp.broadcast_to(jnp.sqrt(ev_ref[...]), (width, width))
     u_t = u.T
@@ -171,8 +165,97 @@
     dm_c = []
     for d in range(1, 4):
         dm_c.append(go(rdma(dmat.at[mine], dmat.at[mine], dm_ss.at[d], dm_rs.at[d], {"dp": plane(d)})))
+    for d in range(1, 4):
+        to = plane(d)
+        w1_c.append(go(rdma(w4.at[:, to], wsc.at[dp], w1_ss.at[d], w1_rs.at[d], {"dp": to})))
+    own_w = pltpu.make_async_copy(w4.at[:, dp], wsc.at[dp], loc.at[slots])
+    own_w.start()
+
     for c in sum_c:
         c.wait_recv()
+    for c in dm_c:
+        c.wait_recv()
+
+    total = (sums[0] + sums[1]) + (sums[2] + sums[3])
+    mean_z, mean_g = total[0:8] / rows, total[8:16] / rows
+    cross, packed = dmat[:mid, :], dmat[mid:, :]
+    flipped = packed.T
+    diag = jnp.broadcast_to(total[16:17, :mid], (mid, mid))
+    sym_ref[:mid, :mid] = jnp.where(
+        row_at < col_at, packed, jnp.where(row_at == col_at, diag, flipped)
+    )
+    sym_ref[mid:, mid:] = jnp.where(row_at < col_at, flipped, packed)
+    sym_ref[:mid, mid:] = cross
+    sym_ref[mid:, :mid] = cross.T
+    outer = jnp.broadcast_to(mean_z[0:1], (width, width)).T * mean_g[0:1]
+    sym = sym_ref[...] - (0.5 * rows) * (outer + outer.T)
+    rotated = dot3(dot3(u_t, sym), u)
+    dsigma = dot3(dot3(u, loewner * rotated), u_t) * (2.0 / rows)
+    mats[2], mats[3] = pair(dsigma)
+    shift[...] = dot3(mean_g, whiten) + dot3(mean_z, dsigma)
+
+    tile = tokens // 4
+
+    @pl.loop(0, 4)
+    def _(t):
+        here = pl.ds(pl.multiple_of(t * tile, tile), tile)
+        g, z = g_ref[here, :], z_ref[here, :]
+        acc = (dot(g, mats[0]) + dot(z, mats[2])) + (dot(g, mats[1]) + dot(z, mats[3]))
+        acc = acc - shift[0:1, :]
+        gz[chan, here, :] = acc.astype(BF16)
+        gzt[:, here] = acc.T.astype(BF16)
+
+    def moves_right(k):
+        slot = 2 * (zc - k) + core
+        return rdma(gz.at[slot], gz.at[slot], rt_ss.at[k], rt_rs.at[k], {"chan": chan + 2})
+
+    def moves_left(k):
+        slot = 2 * (zc + k) + core
+        return rdma(gz.at[slot], gz.at[slot], lt_ss.at[k], lt_rs.at[k], {"chan": chan - 2})
+
+    def from_left(k):
+        slot = 2 * (zc - 1 - k) + core
+        return rdma(gz.at[slot], gz.at[slot], rt_ss.at[k], rt_rs.at[k], {"chan": chan - 2})
+
+    def from_right(k):
+        slot = 2 * (zc + 1 + k) + core
+        return rdma(gz.at[slot], gz.at[slot], lt_ss.at[k], lt_rs.at[k], {"chan": chan + 2})
+
+    def to_mate(block, ss, rs):
+        slot = 2 * block + core
+        return rdma(gz.at[slot], gz.at[slot], ss, rs, {"chan": mate})
+
+    def has_left(k):
+        return zc - 1 - k >= 0
+
+    def has_right(k):
+        return zc + 1 + k <= last
+
+    def sends_right(k):
+        return jnp.logical_and(zc - k >= 0, zc < last)
+
+    def sends_left(k):
+        return jnp.logical_and(zc + k <= last, zc > 0)
+
+    def push(k):
+        pl.when(sends_right(k))(lambda: moves_right(k).start())
+        pl.when(sends_left(k))(lambda: moves_left(k).start())
+
+    def take(k):
+        @pl.when(has_left(k))
+        def _():
+            from_left(k).wait_recv()
+            if k < 2:
+                pl.when(zc < last)(lambda: moves_right(k + 1).start())
+            to_mate(zc - 1 - k, sr_ss.at[k], sr_rs.at[k]).start()
+
+        @pl.when(has_right(k))
+        def _():
+            from_right(k).wait_recv()
+            if k < 2:
+                pl.when(zc > 0)(lambda: moves_left(k + 1).start())
+            to_mate(zc + 1 + k, sl_ss.at[k], sl_rs.at[k]).start()
+
     for c in w1_c:
         c.wait_recv()
     own_w.wait()
@@ -223,95 +306,6 @@
             relay_c.append(go(rdma(ref, ref, wg_ss.at[4 * n + k], wg_rs.at[4 * n + k], where)))
 
     wg_c, relay_c = [], []
-    own_w2.wait()
-    landed(mate)
-    spread(0)
-    for c in dm_c:
-        c.wait_recv()
-
-    total = (sums[0] + sums[1]) + (sums[2] + sums[3])
-    mean_z, mean_g = total[0:8] / rows, total[8:16] / rows
-    cross, packed = dmat[:mid, :], dmat[mid:, :]
-    flipped = packed.T
-    diag = jnp.broadcast_to(total[16:17, :mid], (mid, mid))
-    sym_ref[:mid, :mid] = jnp.where(
-        row_at < col_at, packed, jnp.where(row_at == col_at, diag, flipped)
-    )
-    sym_ref[mid:, mid:] = jnp.where(row_at < col_at, flipped, packed)
-    sym_ref[:mid, mid:] = cross
-    sym_ref[mid:, :mid] = cross.T
-    outer = jnp.broadcast_to(mean_z[0:1], (width, width)).T * mean_g[0:1]
-    sym = sym_ref[...] - (0.5 * rows) * (outer + outer.T)
-    rotated = dot3(dot3(u_t, sym), u)
-    dsigma = dot3(dot3(u, loewner * rotated), u_t) * (2.0 / rows)
-    mats[2], mats[3] = pair(dsigma)
-    shift[...] = dot3(mean_g, whiten) + dot3(mean_z, dsigma)
-
-    tile = tokens // 4
-
-    @pl.loop(0, 4)
-    def _(t):
-        here = pl.ds(pl.multiple_of(t * tile, tile), tile)
-        g, z = g_ref[here, :], z_ref[here, :]
-        acc = (dot(g, mats[0]) + dot(z, mats[2])) + (dot(g, mats[1]) + dot(z, mats[3]))
-        acc = acc - shift[0:1, :]
-        gz[chan, here, :] = acc.astype(BF16)
-        gzt[:, here] = acc.T.astype(BF16)
-
-    def moves_right(k):
-        slot = 2 * (zc - k) + core
-        return rdma(gz.at[slot], gz.at[slot], rt_ss.at[k], rt_rs.at[k], {"chan": chan + 2})
-
-    def moves_left(k):
-        slot = 2 * (zc + k) + core
-        return rdma(gz.at[slot], gz.at[slot], lt_ss.at[k], lt_rs.at[k], {"chan": chan - 2})
-
-    def from_left(k):
-        slot = 2 * (zc - 1 - k) + core
-        return rdma(gz.at[slot], gz.at[slot], rt_ss.at[k], rt_rs.at[k], {"chan": chan - 2})
-
-    def from_right(k):
-        slot = 2 * (zc + 1 + k) + core
-        return rdma(gz.at[slot], gz.at[slot], lt_ss.at[k], lt_rs.at[k], {"chan": chan + 2})
-
-    def to_mate(block, ss, rs):
-        slot = 2 * block + core
-        return rdma(gz.at[slot], gz.at[slot], ss, rs, {"chan": mate})
-
-    def has_left(k):
-        return zc - 1 - k >= 0
-
-    def has_right(k):
-        return zc + 1 + k <= last
-
-    def sends_right(k):
-        return jnp.logical_and(zc - k >= 0, zc < last)
-
-    def sends_left(k):
-        return jnp.logical_and(zc + k <= last, zc > 0)
-
-    def push(k):
-        pl.when(sends_right(k))(lambda: moves_right(k).start())
-        pl.when(sends_left(k))(lambda: moves_left(k).start())
-
-    def take(k):
-        @pl.when(has_left(k))
-        def _():
-            from_left(k).wait_recv()
-            if k < 2:
-                pl.when(zc < last)(lambda: moves_right(k + 1).start())
-            to_mate(zc - 1 - k, sr_ss.at[k], sr_rs.at[k]).start()
-
-        @pl.when(has_right(k))
-        def _():
-            from_right(k).wait_recv()
-            if k < 2:
-                pl.when(zc > 0)(lambda: moves_left(k + 1).start())
-            to_mate(zc + 1 + k, sl_ss.at[k], sl_rs.at[k]).start()
-
-    push(0)
-    own_mate = go(to_mate(zc, sr_ss.at[3], sr_rs.at[3]))
-
     cols = half // 4
 
     def product(n, emit):
@@ -341,12 +335,17 @@
             landed(2 * paired[k] + c)
         spread(k)
 
+    own_w2.wait()
+    landed(mate)
+    spread(0)
     product(2, store(a1s, 0))
     a1_own = go(rdma(a1s.at[0], a1r.at[0], red_ss.at[2], red_rs.at[2], to_x))
     product(3, store(b1s, 0))
     b1_own = go(rdma(b1s.at[0], b1r.at[0], red_ss.at[3], red_rs.at[3], to_y))
+    push(0)
+    own_mate = go(to_mate(zc, sr_ss.at[3], sr_rs.at[3]))
+
     relay(0)
-    take(0)
 
     def store_sum(dst, more):
         def emit(here, value):
@@ -360,6 +359,7 @@
     b1_dg.wait_recv()
     product(5, store_sum(b2s, b1r))
     b2 = go(rdma(b2s, b2r, red_ss.at[5], red_rs.at[5], to_x))
+    take(0)
     next_group(1)
     next_group(2)
     next_group(3)

time: 196 us -> 196 us (level); the launches traced: 193 us -> 196 us
  Pallas kernels: 188 us -> 191 us
    pallas_call x1, Pallas kernels: 188 us -> 191 us  [local_fused(): pl.pallas_call(fused, out_shape=(jax.ShapeDtypeStruct((feats, width), BF1...]
where the time goes in v5:
time: 196 us
  Pallas kernels  191 us (97%)
  local copies, waits for them, and re-layouts  4.52 us (2%)
    pallas_call x1, Pallas kernels, local_fused(): pl.pallas_call(fused, out_shape=(jax.ShapeDtypeStruct((feats, width), BF1...  191 us
    unnamed x4, local copies, waits for them, and re-layouts  4.52 us

profile of v5, /device:TPU:0, one launch (start us, length us, event | category | flops | bytes accessed | tf_op | source)
XLA Modules:
  0.0 196.0 jit_solution(9986605602638744136)
XLA Ops:
  0.6 190.9 %shard_map.77 = (bf16[2048,512]{1,0:T(8,128)(2,1)}, bf16[1024,1024]{1,0:T(8,128)(2,1)}) custom-call(bf16[1024,8192]{1,0:T(8,128)(2,1)} %hid.1, bf16[2,4,256,512]{3,2,1,0:T(8,128)(2,1)} %bitcast.2, bf16[1024,512]{1,0:T(8,128)(2,1)} %z_ref.1, bf16[1024,512]{1,0:T(8,128)(2,1)} %g_ref.1, f32[512,512]{1,0:T(8,128)} %u_ref.1, f32[1,512]{1,0:T(1,128)} %bitcast.3), custom_call_target="tpu_custom_call" | custom-call | flops 20000000000 | bytes 30000000 | tf_op jit(solution)/shard_map/pallas_call | solution.py:434
  191.5 0.0 copy-start
  191.5 3.2 %copy.10 = bf16[2048,512]{1,0:T(8,128)(2,1)} copy(bf16[2048,512]{1,0:T(8,128)(2,1)} %get-tuple-element.4) | data formatting | bytes 4194304
  194.7 0.0 copy-done
  194.7 1.3 copy.11
Async XLA Ops:
  191.5 3.2 %copy-start = (bf16[1024,1024]{1,0:T(8,128)(2,1)S(1)}, bf16[1024,1024]{1,0:T(8,128)(2,1)}, u32[]{:S(2)}) copy-start(bf16[1024,1024]{1,0:T(8,128)(2,1)} %get-tuple-element.5) | copy-start | bytes 6291460

commit v6 on v5

--- a/solution.py
+++ b/solution.py
@@ -274,6 +274,9 @@
     own_w2 = pltpu.make_async_copy(wsc.at[zc, core], wf.at[chan, my_part], loc.at[slots])
     own_w2.start()
 
+    push(0)
+    own_mate = go(to_mate(zc, sr_ss.at[3], sr_rs.at[3]))
+
     to_x, to_y = {"dp": xn}, {"dp": yn}
     half_part = part // 2
 
@@ -342,9 +345,6 @@
     a1_own = go(rdma(a1s.at[0], a1r.at[0], red_ss.at[2], red_rs.at[2], to_x))
     product(3, store(b1s, 0))
     b1_own = go(rdma(b1s.at[0], b1r.at[0], red_ss.at[3], red_rs.at[3], to_y))
-    push(0)
-    own_mate = go(to_mate(zc, sr_ss.at[3], sr_rs.at[3]))
-
     relay(0)
 
     def store_sum(dst, more):
@@ -411,9 +411,29 @@
             value = acc_t[side, :, here] + ref[:, here].astype(F32)
             gw_ref[pl.ds(pl.multiple_of(side * half + start, cols), cols), :] = value.T.astype(BF16)
 
-    for c in relay_c:
+    these = pl.ds(pl.multiple_of(dg * part, part), part)
+    block = tokens // 2
+
+    def share(k, here):
+        e = 2 * paired[k]
+        value = dot(gz[e, here, :], wf[e, these, :], ((1,), (1,)))
+        return value + dot(gz[e + 1, here, :], wf[e + 1, these, :], ((1,), (1,)))
+
+    for c in relay_c[:6]:
         c.wait_recv()
-    hidden_part(dg)
+
+    @pl.loop(0, 2)
+    def _(t):
+        here = pl.ds(pl.multiple_of(t * block, block), block)
+        acc_t[t, :, :part] = share(0, here) + share(1, here) + share(2, here)
+
+    for c in relay_c[6:]:
+        c.wait_recv()
+
+    @pl.loop(0, 2)
+    def _(t):
+        here = pl.ds(pl.multiple_of(t * block, block), block)
+        gh_ref[here, these] = (acc_t[t, :, :part] + share(3, here)).astype(BF16)
 
     for c in sends:
         c.wait_send()

time: 196 us -> 195 us (level)
  Pallas kernels: 191 us -> 189 us
where the time goes in v6:
time: 195 us; the launch traced here: 194 us
  Pallas kernels  189 us (97%)
  local copies, waits for them, and re-layouts  4.52 us (2%)
    pallas_call x1, Pallas kernels, local_fused(): pl.pallas_call(fused, out_shape=(jax.ShapeDtypeStruct((feats, width), BF1...  189 us
    unnamed x4, local copies, waits for them, and re-layouts  4.52 us

profile of v6, /device:TPU:0, one launch (start us, length us, event | category | flops | bytes accessed | tf_op | source)
XLA Modules:
  0.0 194.5 jit_solution(11084491335689195402)
XLA Ops:
  0.6 189.3 %shard_map.77 = (bf16[2048,512]{1,0:T(8,128)(2,1)}, bf16[1024,1024]{1,0:T(8,128)(2,1)}) custom-call(bf16[1024,8192]{1,0:T(8,128)(2,1)} %hid.1, bf16[2,4,256,512]{3,2,1,0:T(8,128)(2,1)} %bitcast.2, bf16[1024,512]{1,0:T(8,128)(2,1)} %z_ref.1, bf16[1024,512]{1,0:T(8,128)(2,1)} %g_ref.1, f32[512,512]{1,0:T(8,128)} %u_ref.1, f32[1,512]{1,0:T(1,128)} %bitcast.3), custom_call_target="tpu_custom_call" | custom-call | flops 20000000000 | bytes 30000000 | tf_op jit(solution)/shard_map/pallas_call | solution.py:454
  189.9 0.0 copy-start
  189.9 3.2 %copy.10 = bf16[2048,512]{1,0:T(8,128)(2,1)} copy(bf16[2048,512]{1,0:T(8,128)(2,1)} %get-tuple-element.4) | data formatting | bytes 4194304
  193.1 0.0 copy-done
  193.1 1.3 copy.11
Async XLA Ops:
  189.9 3.2 %copy-start = (bf16[1024,1024]{1,0:T(8,128)(2,1)S(1)}, bf16[1024,1024]{1,0:T(8,128)(2,1)}, u32[]{:S(2)}) copy-start(bf16[1024,1024]{1,0:T(8,128)(2,1)} %get-tuple-element.5) | copy-start | bytes 6291460
